TPU v7x, 32 devices: a whole 2x2x4 slice. The times are simulated.
32 devices in a mesh: row: 4 (over x, core), col: 8 (over z, y).
Axes of the slice: x: 2, y: 2, z: 4, core: 2. Of those that a mesh axis runs over, the one named last changes fastest.
Arguments:
- features: float32 [3, 4, 512, 768], P(None, 'row'), may hold values from -6 to 6
- ridge: float32 [3, 4, 512], P(None, 'row'), may hold values from 0.5 to 4
Outputs:
- schur: float32 [3, 4, 512, 6, 8, 128], P(None, 'row', None, None, 'col')
- panel: float32 [3, 4, 512, 512], P(None, 'row')
All inputs are finite; a program needn't handle non-finite values.
Results may differ from a plain program's by a relative error of at most 0.00017.
Values sent between devices are 32-bit elements; how exact they have to be, the bound alone decides.
A program may use at most 64 MiB of HBM per device.

v0:
```python
import functools

import jax
import jax.numpy as jnp
from jax import lax
from jax.experimental import pallas as pl
from jax.experimental.pallas import tpu as pltpu
from jax.sharding import PartitionSpec as P

CB = 128
STEP = 4
HIGHEST = lax.Precision.HIGHEST
MESH = pl.DeviceIdType.MESH


def dot_t(a, b, precision=None):
    return lax.dot_general(
        a, b, (((1,), (1,)), ((), ())), precision=precision, preferred_element_type=jnp.float32
    )


def split(x):
    hi = x.astype(jnp.bfloat16)
    return hi, (x - hi.astype(jnp.float32)).astype(jnp.bfloat16)


def dot3_t(a, b):
    return dot_t(a[0], b[0]) + (dot_t(a[0], b[1]) + dot_t(a[1], b[0]))


def kernel_value(inner, width):
    return jnp.square(inner * (1.0 / width) + 1.0)


def factor_inverse(w):
    n = w.shape[0]
    lanes = lax.broadcasted_iota(jnp.int32, (1, n), 1)
    rows_out = []
    for j in range(0, n, STEP):
        top = j // 8 * 8
        if w.shape[0] != n - top:
            w = w[8:, :]
        at = j - top
        ids = top + lax.broadcasted_iota(jnp.int32, w.shape, 0)
        all_lanes = lax.broadcasted_iota(jnp.int32, w.shape, 1)
        cols = [jnp.broadcast_to(w[:, j + k : j + k + 1], w.shape) for k in range(STEP)]
        inside = (all_lanes >= j) & (all_lanes < j + STEP) & (ids >= j)
        w = jnp.where(inside, jnp.where(ids == all_lanes, 1.0, 0.0), w)
        rows = [w[at + k : at + k + 1, :] for k in range(STEP)]
        for k in range(STEP):
            piv = cols[k][at + k : at + k + 1, :]
            inv = 1.0 / piv
            scaled = rows[k] * inv
            for m in range(k + 1, STEP):
                rows[m] = rows[m] - cols[k][at + m : at + m + 1, :] * scaled
                cols[m] = cols[m] - cols[k] * (cols[m][at + k : at + k + 1, :] * inv)
            w = w - jnp.where(ids > j + k, cols[k], 0.0) * scaled
            rows_out.append(jnp.where(lanes <= j + k, rows[k] * lax.rsqrt(piv), 0.0))
    return jnp.concatenate(rows_out, axis=0)


def factor_kernel(
    shape, n_row, n_col, feat, ridge0, linv, buf, ridge_p, kp_s,
    local_sem, send_sem, relay_sem, recv_sem, ridge_send, ridge_recv,
):
    width, depth, chunks, slots = shape
    r = lax.axis_index("row")
    q = lax.axis_index("col")
    mate = r + 1 - 2 * (r % 2)
    parity = r % 2
    pair = r // 2
    n_pair = n_row // 2

    barrier = pltpu.get_barrier_semaphore()
    for d in range(1, n_row):
        pl.semaphore_signal(
            barrier, inc=1, device_id=(lax.rem(r + d, n_row), q), device_id_type=MESH
        )
    pl.semaphore_wait(barrier, n_row - 1)

    def place(u):
        if u < chunks:
            return 0, 0, u * CB
        first = ((u - chunks) * n_col + q) * CB
        tile = first // width
        return tile % n_row, tile // n_row, first % width

    def source(u):
        owner, tile, off = place(u)
        return feat.at[tile, pl.ds(pl.multiple_of(off, CB), CB), :]

    def dest(u):
        return buf.at[pl.ds(u * CB, CB), :]

    def send(u, d):
        to = mate if d == 0 else 2 * lax.rem(pair + d, n_pair) + parity
        return pltpu.make_async_remote_copy(
            src_ref=source(u), dst_ref=dest(u), send_sem=send_sem.at[u, d],
            recv_sem=recv_sem.at[u], device_id=(to, q), device_id_type=MESH,
        )

    def forward(u):
        return pltpu.make_async_remote_copy(
            src_ref=dest(u), dst_ref=dest(u), send_sem=relay_sem.at[u],
            recv_sem=recv_sem.at[u], device_id=(mate, q), device_id_type=MESH,
        )

    def own(u):
        return pltpu.make_async_copy(source(u), dest(u), local_sem.at[u])

    def start(u):
        @pl.when(place(u)[0] == r)
        def _():
            for d in range(1, n_pair):
                send(u, d).start()
            send(u, 0).start()
            own(u).start()

    def is_relay(u):
        owner = place(u)[0]
        return (owner != r) & (owner % 2 == parity)

    def arrive(u):
        @pl.when(place(u)[0] == r)
        def _():
            own(u).wait()

        @pl.when(place(u)[0] != r)
        def _():
            forward(u).wait_recv()

        @pl.when(is_relay(u))
        def _():
            forward(u).start()

    def finish(u):
        @pl.when(place(u)[0] == r)
        def _():
            for d in range(n_pair):
                send(u, d).wait_send()

        @pl.when(is_relay(u))
        def _():
            forward(u).wait_send()

    def ridge_copy(d):
        return pltpu.make_async_remote_copy(
            src_ref=ridge0, dst_ref=ridge_p, send_sem=ridge_send.at[d], recv_sem=ridge_recv,
            device_id=(lax.rem(r + d, n_row), q), device_id_type=MESH,
        )

    @pl.when(r == 0)
    def _():
        for d in range(1, n_row):
            ridge_copy(d).start()
        ridge_p[...] = ridge0[...]

    for u in range(chunks):
        start(u)

    @pl.when(r != 0)
    def _():
        ridge_copy(1).wait_recv()

    linv[...] = jnp.zeros_like(linv)
    late = chunks + (slots + 1) // 2
    for p in range(chunks):
        arrive(p)
        if p == 0:
            for u in range(chunks, chunks + slots):
                start(u)
        if p == chunks - 1:
            for u in range(chunks, late):
                arrive(u)
        here = slice(p * CB, (p + 1) * CB)
        upto = (p + 1) * CB
        mine = buf[here, :]
        for c in range(p + 1):
            there = slice(c * CB, (c + 1) * CB)
            kp_s[p % 2, :, there] = kernel_value(dot_t(mine, buf[there, :], HIGHEST), depth)
        eye = lax.broadcasted_iota(jnp.int32, (CB, CB), 0) == lax.broadcasted_iota(
            jnp.int32, (CB, CB), 1
        )
        s = kp_s[p % 2, :, here] + jnp.where(eye, ridge_p[:, here], 0.0)
        if p > 0:
            before = linv[0 : p * CB, 0 : p * CB]
            low = dot_t(kp_s[p % 2, :, 0 : p * CB], before, HIGHEST)
            s = s - dot_t(low, low, HIGHEST)
            across = jnp.dot(low, before, precision=HIGHEST, preferred_element_type=jnp.float32)
        inv = factor_inverse(s)
        linv[here, here] = inv
        if p > 0:
            linv[here, 0 : p * CB] = -jnp.dot(
                inv, across, precision=HIGHEST, preferred_element_type=jnp.float32
            )
    for u in range(late, chunks + slots):
        arrive(u)
    for u in range(chunks + slots):
        finish(u)

    @pl.when(r == 0)
    def _():
        for d in range(1, n_row):
            ridge_copy(d).wait_send()


def schur_kernel(
    shape, n_row, n_col, place, rows, buf, linv, ridge, schur, panel, fh, fl, lh, ll, ch, cl
):
    width, depth, slots, per_tile = shape
    r = place[0]
    q = place[1]
    i = pl.program_id(0)
    step_rows = rows.shape[0]
    n_cols = slots * CB

    @pl.when(i == 0)
    def _():
        h, l = split(buf[...])
        fh[...] = h
        fl[...] = l
        h, l = split(linv[...])
        lh[...] = h
        ll[...] = l
        for s in range(slots):
            mine = slice(width + s * CB, width + (s + 1) * CB)
            k = kernel_value(
                dot3_t((fh[mine, :], fl[mine, :]), (fh[0:width, :], fl[0:width, :])), depth
            )
            first = (s * n_col + q) * CB
            delta = lax.broadcasted_iota(jnp.int32, k.shape, 1) - lax.broadcasted_iota(
                jnp.int32, k.shape, 0
            )
            k = k + jnp.where(delta == first, ridge[ridge.shape[0] - 1], 0.0)
            h, l = split(dot3_t(split(k), (lh[...], ll[...])))
            ch[s * CB : (s + 1) * CB, :] = h
            cl[s * CB : (s + 1) * CB, :] = l

    x = split(rows[...])
    t = i // per_tile
    first = (t * n_row + r) * width + (i % per_tile) * step_rows
    k = kernel_value(dot3_t(x, (fh[0:width, :], fl[0:width, :])), depth)
    delta = lax.broadcasted_iota(jnp.int32, k.shape, 1) - lax.broadcasted_iota(
        jnp.int32, k.shape, 0
    )
    k = k + jnp.where(delta == first, ridge[ridge.shape[0] - 1], 0.0)
    low = dot3_t(split(k), (lh[...], ll[...]))
    panel[...] = low
    low = split(low)
    delta = lax.broadcasted_iota(jnp.int32, (step_rows, CB), 0) - lax.broadcasted_iota(
        jnp.int32, (step_rows, CB), 1
    )
    wide = 2 if slots % 2 == 0 else 1
    for s0 in range(0, slots, wide):
        mine = slice(width + s0 * CB, width + (s0 + wide) * CB)
        these = slice(s0 * CB, (s0 + wide) * CB)
        value = kernel_value(dot3_t(x, (fh[mine, :], fl[mine, :])), depth) - dot3_t(
            low, (ch[these, :], cl[these, :])
        )
        for w in range(wide):
            s = s0 + w
            col = (s * n_col + q) * CB
            off = pl.multiple_of(col % width, CB)
            extra = jnp.where(delta == col - first, ridge[t, :, pl.ds(off, CB)], 0.0)
            part = value[:, w * CB : (w + 1) * CB] + extra
            if slots == 1:
                schur[...] = part
            else:
                schur[pl.ds(s, step_rows, stride=slots), :] = part


def per_device(features, ridge):
    tiles, _, width, depth = features.shape
    n_row = lax.axis_size("row")
    n_col = lax.axis_size("col")
    slots = tiles * n_row * width // (n_col * CB)
    chunks = width // CB
    units = chunks + slots
    feat = features.reshape(tiles, width, depth)
    ridge_rows = ridge.reshape(tiles, width)
    vmem = pl.BlockSpec(memory_space=pltpu.VMEM)
    linv, buf, ridge_p = pl.pallas_call(
        functools.partial(factor_kernel, (width, depth, chunks, slots), n_row, n_col),
        out_shape=(
            jax.ShapeDtypeStruct((width, width), jnp.float32),
            jax.ShapeDtypeStruct((units * CB, depth), jnp.float32),
            jax.ShapeDtypeStruct((1, width), jnp.float32),
        ),
        in_specs=[pl.BlockSpec(memory_space=pl.ANY), vmem],
        out_specs=(vmem, vmem, vmem),
        scratch_shapes=[
            pltpu.VMEM((2, CB, width), jnp.float32),
            pltpu.SemaphoreType.DMA((units,)),
            pltpu.SemaphoreType.DMA((units, n_row // 2)),
            pltpu.SemaphoreType.DMA((units,)),
            pltpu.SemaphoreType.DMA((units,)),
            pltpu.SemaphoreType.DMA((n_row,)),
            pltpu.SemaphoreType.DMA,
        ],
        compiler_params=pltpu.CompilerParams(
            collective_id=0, has_side_effects=True, vmem_limit_bytes=40 * 2**20
        ),
    )(feat, ridge_rows[0:1])

    place = jnp.stack([lax.axis_index("row"), lax.axis_index("col")])
    ridges = jnp.concatenate([ridge_rows, ridge_p], axis=0)[:, None, :]
    step_rows = 256
    per_tile = width // step_rows
    whole = lambda shape: pl.BlockSpec(shape, lambda i, place: (0,) * len(shape))
    schur, panel = pl.pallas_call(
        functools.partial(schur_kernel, (width, depth, slots, per_tile), n_row, n_col),
        out_shape=(
            jax.ShapeDtypeStruct((tiles * width * slots, CB), jnp.float32),
            jax.ShapeDtypeStruct((tiles * width, width), jnp.float32),
        ),
        grid_spec=pltpu.PrefetchScalarGridSpec(
            num_scalar_prefetch=1,
            grid=(tiles * per_tile,),
            in_specs=[
                pl.BlockSpec((step_rows, depth), lambda i, place: (i, 0)),
                whole((units * CB, depth)),
                whole((width, width)),
                whole((tiles + 1, 1, width)),
            ],
            out_specs=[
                pl.BlockSpec((step_rows * slots, CB), lambda i, place: (i, 0)),
                pl.BlockSpec((step_rows, width), lambda i, place: (i, 0)),
            ],
            scratch_shapes=[
                pltpu.VMEM((units * CB, depth), jnp.bfloat16),
                pltpu.VMEM((units * CB, depth), jnp.bfloat16),
                pltpu.VMEM((width, width), jnp.bfloat16),
                pltpu.VMEM((width, width), jnp.bfloat16),
                pltpu.VMEM((slots * CB, width), jnp.bfloat16),
                pltpu.VMEM((slots * CB, width), jnp.bfloat16),
            ],
        ),
        compiler_params=pltpu.CompilerParams(vmem_limit_bytes=48 * 2**20),
    )(place, features.reshape(tiles * width, depth), buf, linv, ridges)
    return (
        schur.reshape(tiles, 1, width, slots, 1, CB),
        panel.reshape(tiles, 1, width, width),
    )


def solution(mesh):
    in_specs = (P(None, "row", None, None), P(None, "row", None))
    out_specs = (P(None, "row", None, None, "col", None), P(None, "row", None, None))
    return jax.shard_map(
        per_device, mesh=mesh, in_specs=in_specs, out_specs=out_specs, check_vma=False
    )
```

profile of v0, /device:TPU:22, one launch (start us, length us, event | category | flops | bytes accessed | tf_op | source)
XLA Modules:
  0.0 79.0 jit_solution(9893992128938684479)
XLA Ops:
  0.6 0.1 pad_add_fusion.place
  0.7 0.7 slice_bitcast_fusion.ridge0
  1.4 0.7 copy.10
  2.1 0.0 copy-start
  2.1 2.3 %copy-done = f32[3,1,512,768]{3,2,1,0:T(8,128)S(1)} copy-done((f32[3,1,512,768]{3,2,1,0:T(8,128)S(1)}, f32[3,1,512,768]{3,2,1,0:T(8,128)}, u32[]{:S(2)}) %copy-start) | copy-done | bytes 4718616
  4.4 45.9 %shard_map.41 = (f32[512,512]{1,0:T(8,128)S(1)}, f32[1280,768]{1,0:T(8,128)S(1)}, f32[1,512]{1,0:T(1,128)S(1)}) custom-call(f32[3,512,768]{2,1,0:T(8,128)S(1)} %bitcast.14, f32[1,512]{1,0:T(1,128)S(1)} %slice_bitcast_fusion.ridge0), custom_call_target="tpu_custom_call" | custom-call | tf_op jit(solution)/shard_map/pallas_call | solution.py:282
  50.4 28.7 %shard_map.42 = (f32[9216,128]{1,0:T(8,128)}, f32[1536,512]{1,0:T(8,128)}) custom-call(s32[2]{0:T(128)S(1)} %pad_add_fusion.place, f32[1536,768]{1,0:T(8,128)} %bitcast.13, f32[1280,768]{1,0:T(8,128)S(1)} %get-tuple-element.7.buf, f32[512,512]{1,0:T(8,128)S(1)} %get-tuple-element.8.linv, f32[4,1,512]{2,1,0:T(1,128)S(1)} %broadcast_in_dim.3.ridge), custom_call_target="tpu_custom_call" | custom-call | tf_op jit(solution)/shard_map/pallas_call | solution.py:310
  (2 shorter events, 0.0 us)
Async XLA Ops:
  2.1 2.3 %copy-start = (f32[3,1,512,768]{3,2,1,0:T(8,128)S(1)}, f32[3,1,512,768]{3,2,1,0:T(8,128)}, u32[]{:S(2)}) copy-start(f32[3,1,512,768]{3,2,1,0:T(8,128)} %param.2) | copy-start | bytes 14155780
where the time goes:
time: 79.3 us; the launch traced here: 79 us
  Pallas kernels  74.6 us (94%)
  local copies, waits for them, and re-layouts  3.72 us (5%)
    pallas_call x1, Pallas kernels, per_device(): pl.pallas_call(functools.partial(factor_kernel, (width, depth, chunks, sl...  45.9 us
    pallas_call x1, Pallas kernels, per_device(): pl.pallas_call(functools.partial(schur_kernel, (width, depth, slots, per_...  28.7 us
    unnamed x3, local copies, waits for them, and re-layouts  3.03 us

commit v1 on v0

--- a/solution.py
+++ b/solution.py
@@ -8,7 +8,7 @@
 from jax.sharding import PartitionSpec as P
 
 CB = 128
-STEP = 4
+STEP = 8
 HIGHEST = lax.Precision.HIGHEST
 MESH = pl.DeviceIdType.MESH
 
@@ -24,19 +24,25 @@
     return hi, (x - hi.astype(jnp.float32)).astype(jnp.bfloat16)
 
 
-def dot3_t(a, b):
-    return dot_t(a[0], b[0]) + (dot_t(a[0], b[1]) + dot_t(a[1], b[0]))
+def dot3(a, b):
+    return jnp.dot(
+        jnp.concatenate([a[0], a[0], a[1]], axis=1),
+        jnp.concatenate([b[0], b[1], b[0]], axis=0),
+        preferred_element_type=jnp.float32,
+    )
 
 
 def kernel_value(inner, width):
     return jnp.square(inner * (1.0 / width) + 1.0)
 
 
-def factor_inverse(w):
+def factor_inverse(w, midway):
     n = w.shape[0]
     lanes = lax.broadcasted_iota(jnp.int32, (1, n), 1)
     rows_out = []
     for j in range(0, n, STEP):
+        if j == n // 2:
+            midway()
         top = j // 8 * 8
         if w.shape[0] != n - top:
             w = w[8:, :]
@@ -163,15 +169,16 @@
         ridge_copy(1).wait_recv()
 
     linv[...] = jnp.zeros_like(linv)
-    late = chunks + (slots + 1) // 2
+
+    def arrive_cols():
+        for u in range(chunks, chunks + slots):
+            arrive(u)
+
     for p in range(chunks):
         arrive(p)
-        if p == 0:
+        if p == min(1, chunks - 1):
             for u in range(chunks, chunks + slots):
                 start(u)
-        if p == chunks - 1:
-            for u in range(chunks, late):
-                arrive(u)
         here = slice(p * CB, (p + 1) * CB)
         upto = (p + 1) * CB
         mine = buf[here, :]
@@ -187,14 +194,12 @@
             low = dot_t(kp_s[p % 2, :, 0 : p * CB], before, HIGHEST)
             s = s - dot_t(low, low, HIGHEST)
             across = jnp.dot(low, before, precision=HIGHEST, preferred_element_type=jnp.float32)
-        inv = factor_inverse(s)
+        inv = factor_inverse(s, arrive_cols if p == chunks - 1 else lambda: None)
         linv[here, here] = inv
         if p > 0:
             linv[here, 0 : p * CB] = -jnp.dot(
                 inv, across, precision=HIGHEST, preferred_element_type=jnp.float32
             )
-    for u in range(late, chunks + slots):
-        arrive(u)
     for u in range(chunks + slots):
         finish(u)
 
@@ -212,50 +217,53 @@
     q = place[1]
     i = pl.program_id(0)
     step_rows = rows.shape[0]
-    n_cols = slots * CB
+    wide = 2 if slots % 2 == 0 else 1
 
     @pl.when(i == 0)
     def _():
-        h, l = split(buf[...])
+        h, l = split(buf[...].T)
         fh[...] = h
         fl[...] = l
-        h, l = split(linv[...])
+        h, l = split(linv[...].T)
         lh[...] = h
         ll[...] = l
-        for s in range(slots):
-            mine = slice(width + s * CB, width + (s + 1) * CB)
-            k = kernel_value(
-                dot3_t((fh[mine, :], fl[mine, :]), (fh[0:width, :], fl[0:width, :])), depth
-            )
-            first = (s * n_col + q) * CB
-            delta = lax.broadcasted_iota(jnp.int32, k.shape, 1) - lax.broadcasted_iota(
-                jnp.int32, k.shape, 0
-            )
-            k = k + jnp.where(delta == first, ridge[ridge.shape[0] - 1], 0.0)
-            h, l = split(dot3_t(split(k), (lh[...], ll[...])))
-            ch[s * CB : (s + 1) * CB, :] = h
-            cl[s * CB : (s + 1) * CB, :] = l
+        low_inv = split(linv[...])
+        lead = split(buf[0:width, :])
+        delta = lax.broadcasted_iota(jnp.int32, (width, CB), 0) - lax.broadcasted_iota(
+            jnp.int32, (width, CB), 1
+        )
+        for s0 in range(0, slots, wide):
+            mine = slice(width + s0 * CB, width + (s0 + wide) * CB)
+            k = kernel_value(dot3(lead, (fh[:, mine], fl[:, mine])), depth)
+            parts = []
+            for w in range(wide):
+                col = ((s0 + w) * n_col + q) * CB
+                off = pl.multiple_of(col % width, CB)
+                extra = jnp.where(delta == col, ridge[ridge.shape[0] - 1, :, pl.ds(off, CB)], 0.0)
+                parts.append(k[:, w * CB : (w + 1) * CB] + extra)
+            h, l = split(dot3(low_inv, split(jnp.concatenate(parts, axis=1))))
+            ch[:, s0 * CB : (s0 + wide) * CB] = h
+            cl[:, s0 * CB : (s0 + wide) * CB] = l
 
     x = split(rows[...])
     t = i // per_tile
     first = (t * n_row + r) * width + (i % per_tile) * step_rows
-    k = kernel_value(dot3_t(x, (fh[0:width, :], fl[0:width, :])), depth)
+    k = kernel_value(dot3(x, (fh[:, 0:width], fl[:, 0:width])), depth)
     delta = lax.broadcasted_iota(jnp.int32, k.shape, 1) - lax.broadcasted_iota(
         jnp.int32, k.shape, 0
     )
     k = k + jnp.where(delta == first, ridge[ridge.shape[0] - 1], 0.0)
-    low = dot3_t(split(k), (lh[...], ll[...]))
+    low = dot3(split(k), (lh[...], ll[...]))
     panel[...] = low
     low = split(low)
     delta = lax.broadcasted_iota(jnp.int32, (step_rows, CB), 0) - lax.broadcasted_iota(
         jnp.int32, (step_rows, CB), 1
     )
-    wide = 2 if slots % 2 == 0 else 1
     for s0 in range(0, slots, wide):
         mine = slice(width + s0 * CB, width + (s0 + wide) * CB)
         these = slice(s0 * CB, (s0 + wide) * CB)
-        value = kernel_value(dot3_t(x, (fh[mine, :], fl[mine, :])), depth) - dot3_t(
-            low, (ch[these, :], cl[these, :])
+        value = kernel_value(dot3(x, (fh[:, mine], fl[:, mine])), depth) - dot3(
+            low, (ch[:, these], cl[:, these])
         )
         for w in range(wide):
             s = s0 + w
@@ -327,12 +335,12 @@
                 pl.BlockSpec((step_rows, width), lambda i, place: (i, 0)),
             ],
             scratch_shapes=[
-                pltpu.VMEM((units * CB, depth), jnp.bfloat16),
-                pltpu.VMEM((units * CB, depth), jnp.bfloat16),
+                pltpu.VMEM((depth, units * CB), jnp.bfloat16),
+                pltpu.VMEM((depth, units * CB), jnp.bfloat16),
                 pltpu.VMEM((width, width), jnp.bfloat16),
                 pltpu.VMEM((width, width), jnp.bfloat16),
-                pltpu.VMEM((slots * CB, width), jnp.bfloat16),
-                pltpu.VMEM((slots * CB, width), jnp.bfloat16),
+                pltpu.VMEM((width, slots * CB), jnp.bfloat16),
+                pltpu.VMEM((width, slots * CB), jnp.bfloat16),
             ],
         ),
         compiler_params=pltpu.CompilerParams(vmem_limit_bytes=48 * 2**20),

time: 79.3 us -> 74.6 us (0.941)
  Pallas kernels: 74.6 us -> 69.9 us
    pallas_call x1, Pallas kernels: 45.9 us -> 43.2 us  [per_device(): pl.pallas_call(functools.partial(factor_kernel, (width, depth, chunks, sl...]
    pallas_call x1, Pallas kernels: 28.7 us -> 26.7 us  [per_device(): pl.pallas_call(functools.partial(schur_kernel, (width, depth, slots, per_...]
where the time goes in v1:
time: 74.6 us; the launch traced here: 74.4 us
  Pallas kernels  69.9 us (94%)
  local copies, waits for them, and re-layouts  3.72 us (5%)
    pallas_call x1, Pallas kernels, per_device(): pl.pallas_call(functools.partial(factor_kernel, (width, depth, chunks, sl...  43.2 us
    pallas_call x1, Pallas kernels, per_device(): pl.pallas_call(functools.partial(schur_kernel, (width, depth, slots, per_...  26.7 us
    unnamed x3, local copies, waits for them, and re-layouts  3.03 us

profile of v1, /device:TPU:22, one launch (start us, length us, event | category | flops | bytes accessed | tf_op | source)
XLA Modules:
  0.0 74.4 jit_solution(11241320204298111253)
XLA Ops:
  0.6 0.1 pad_add_fusion.place
  0.7 0.7 slice_bitcast_fusion.ridge0
  1.4 0.7 copy.10
  2.1 0.0 copy-start
  2.1 2.3 %copy-done = f32[3,1,512,768]{3,2,1,0:T(8,128)S(1)} copy-done((f32[3,1,512,768]{3,2,1,0:T(8,128)S(1)}, f32[3,1,512,768]{3,2,1,0:T(8,128)}, u32[]{:S(2)}) %copy-start) | copy-done | bytes 4718616
  4.4 43.2 %shard_map.41 = (f32[512,512]{1,0:T(8,128)S(1)}, f32[1280,768]{1,0:T(8,128)S(1)}, f32[1,512]{1,0:T(1,128)S(1)}) custom-call(f32[3,512,768]{2,1,0:T(8,128)S(1)} %bitcast.14, f32[1,512]{1,0:T(1,128)S(1)} %slice_bitcast_fusion.ridge0), custom_call_target="tpu_custom_call" | custom-call | tf_op jit(solution)/shard_map/pallas_call | solution.py:290
  47.7 26.7 %shard_map.42 = (f32[9216,128]{1,0:T(8,128)}, f32[1536,512]{1,0:T(8,128)}) custom-call(s32[2]{0:T(128)S(1)} %pad_add_fusion.place, f32[1536,768]{1,0:T(8,128)} %bitcast.13, f32[1280,768]{1,0:T(8,128)S(1)} %get-tuple-element.7.buf, f32[512,512]{1,0:T(8,128)S(1)} %get-tuple-element.8.linv, f32[4,1,512]{2,1,0:T(1,128)S(1)} %broadcast_in_dim.3.ridge), custom_call_target="tpu_custom_call" | custom-call | tf_op jit(solution)/shard_map/pallas_call | solution.py:318
  (2 shorter events, 0.0 us)
Async XLA Ops:
  2.1 2.3 %copy-start = (f32[3,1,512,768]{3,2,1,0:T(8,128)S(1)}, f32[3,1,512,768]{3,2,1,0:T(8,128)}, u32[]{:S(2)}) copy-start(f32[3,1,512,768]{3,2,1,0:T(8,128)} %param.2) | copy-start | bytes 14155780
